TPU v7x, 32 devices: a whole 2x2x4 slice. The times are simulated.
32 devices in a mesh: groups: 2 (over x), az: 16 (over z, y, core).
Axes of the slice: x: 2, y: 2, z: 4, core: 2. Of those that a mesh axis runs over, the one named last changes fastest.
Arguments:
- surface_nodes: bfloat16 [8, 16, 128, 2304], P('groups', 'az'), parts along dimension 0, may hold values from -6 to 6
- amplitudes: bfloat16 [16, 256, 4, 16, 128], P('groups', None, None, 'az'), parts along dimension 0, may hold values from -0.0625 to 0.0625
- block_offsets: int32 [16, 32], P('az', 'groups'), parts along dimension 1, may hold values from -1 to 248, as said below
- welch_first: int32 [512], P(('groups', 'az')), parts along dimension 0, may hold values from 0 to 512
Outputs:
- pressure: float32 [512, 2048], P(('groups', 'az')), parts along dimension 0
- spectra: float32 [512, 512], P(('groups', 'az')), parts along dimension 0
There are 2 independent parts, one for each index of `groups`. A program takes and returns all parts, laid end to end along the dimension named above; each array names one. Nothing has to cross between parts.
Inputs may be any that keep to these rules, and one draw needn't show every extreme that they name: `block_offsets`: an entry of -1 marks a panel column and observer block whose contribution is left out; any other entry is the pair's coarse retarded-time offset in samples.
All inputs are finite; a program needn't handle non-finite values.
Results may differ from a plain program's by a relative error of at most 0.0003.
Values may be sent and summed in bfloat16 or wider, within the bound.
A program may use at most 64 MiB of HBM per device.

v0:
```python
import jax
import jax.numpy as jnp
from jax import lax
from jax.sharding import PartitionSpec as P

NAXIAL = 128
NO = 256
KTAPS = 8
HEAD = 256
SEG = 1024
NSEG = 2
NSAMP = 2048


def shifted(block, axis, distance):
    devices = range(lax.axis_size(axis))
    route = [((i - distance) % len(devices), i) for i in devices]
    return lax.ppermute(block, axis, route)


def pair_term(node_list, amp_rows, offset, length):
    observers = amp_rows.shape[0] // KTAPS

    def compute():
        delayed = jnp.zeros((amp_rows.shape[0], length + HEAD), jnp.float32)
        for node_rows in node_list:
            delayed = delayed + jnp.dot(amp_rows, node_rows, preferred_element_type=jnp.float32)
        delayed = (0.5 * delayed).reshape(KTAPS, observers, length + HEAD)
        summed = jnp.zeros((observers, length), jnp.float32)
        for tap_index in range(KTAPS):
            summed = summed + lax.dynamic_slice_in_dim(
                delayed[tap_index], HEAD - offset - tap_index, length, axis=1
            )
        return summed

    def skipped():
        return jnp.zeros((observers, length), jnp.float32)

    return lax.cond(offset >= 0, compute, skipped)


def welch_basis():
    sample_index = jnp.arange(SEG, dtype=jnp.int32)
    frequency = jnp.arange(SEG // 2, dtype=jnp.int32)
    phase_index = sample_index[:, None] * frequency[None, :] % SEG
    angles = 2.0 * jnp.pi / SEG * phase_index.astype(jnp.float32)
    window = 0.5 - 0.5 * jnp.cos(2.0 * jnp.pi / SEG * sample_index.astype(jnp.float32))
    dft_basis = jnp.concatenate([jnp.cos(angles), -jnp.sin(angles)], axis=1) * window[:, None]
    return (dft_basis, jnp.sum(window * window))


def welch_spectra(pressure, welch_first):
    dft_basis, energy = welch_basis()
    half_seg = SEG // 2

    def slice_series(series, start_at):
        return jnp.stack(
            [
                lax.dynamic_slice_in_dim(series, start_at + segment_id * half_seg, SEG)
                for segment_id in range(NSEG)
            ]
        )

    segments = jax.vmap(slice_series)(pressure, welch_first)
    num_rows = pressure.shape[0]
    coeffs = jnp.dot(
        segments.reshape(num_rows * NSEG, SEG),
        dft_basis,
        precision=lax.Precision.HIGHEST,
        preferred_element_type=jnp.float32,
    )
    power = coeffs[:, :half_seg] ** 2 + coeffs[:, half_seg:] ** 2
    return jnp.mean(power.reshape(num_rows, NSEG, half_seg), axis=1) / energy


def on_device(surface_nodes, amplitudes, block_offsets, welch_first):
    cycle_size = lax.axis_size("az")
    position = lax.axis_index("az")
    observers = NO // cycle_size
    own_rows = surface_nodes.reshape(4 * NAXIAL, surface_nodes.shape[-1])
    own_table = amplitudes.reshape(KTAPS, NO, 4 * NAXIAL)
    own_offsets = block_offsets[0]
    following = shifted(surface_nodes, "az", -1)
    next_rows = following.reshape(4 * NAXIAL, following.shape[-1])
    sources = [(own_table, own_offsets, [own_rows, next_rows])]

    def observer_term(obs_block, length):
        amp_table, offset_row, node_list = sources[0]
        chosen = lax.dynamic_slice_in_dim(amp_table, obs_block * observers, observers, axis=1)
        summed = pair_term(
            node_list, chosen.reshape(KTAPS * observers, 4 * NAXIAL), offset_row[obs_block], length
        )
        return summed

    def advance(step_id, carried):
        obs_block = (position - 1 - step_id) % cycle_size
        return shifted(carried + observer_term(obs_block, NSAMP), "az", 1)

    carried = lax.fori_loop(0, cycle_size - 1, advance, jnp.zeros((observers, NSAMP), jnp.float32))
    pressure = carried + observer_term(position, NSAMP)
    spectra = welch_spectra(pressure, welch_first)
    return (pressure, spectra)


def solution(mesh):
    placed = (
        P("groups", "az", None, None),
        P("groups", None, None, "az", None),
        P("az", "groups"),
        P(("groups", "az")),
    )
    return jax.shard_map(
        on_device,
        mesh=mesh,
        in_specs=placed,
        out_specs=(P(("groups", "az"), None), P(("groups", "az"), None)),
        check_vma=False,
    )
```

profile of v0, /device:TPU:0, one launch (start us, length us, event | category | flops | bytes accessed | tf_op | source)
XLA Modules:
  0.0 494.9 jit_solution(12333337622952736739)
XLA Ops:
  12.3 9.2 %sine_negate_fusion = (f32[1024,512]{1,0:T(8,128)}, f32[1024,512]{1,0:T(8,128)}) fusion(), kind=kLoop, calls=%fused_computation.21 | loop fusion | flops 7864320 | bytes 4194304 | tf_op jit(solution)/shard_map/neg | solution.py:48
  21.5 11.3 %collective-permute-done.1 = bf16[4,1,128,2304]{3,2,1,0:T(8,128)(2,1)} collective-permute-done((bf16[4,1,128,2304]{3,2,1,0:T(8,128)(2,1)}, bf16[4,1,128,2304]{3,2,1,0:T(8,128)(2,1)}, u32[]{:S(2)}, u32[]{:S(2)}) %collective-permute-start.1) | collective-permute-done | bytes 2359328 | tf_op jit(solution)/shard_map/ppermute | solution.py:18
  32.8 14.9 %conditional.2 = (f32[16,2048]{1,0:T(8,128)}) conditional(s32[]{:T(128)} %convert_element_type.27, () %tuple.57, (s32[]{:T(128)}, bf16[8,256,512]{2,1,0:T(8,128)(2,1)}, bf16[512,2304]{1,0:T(8,128)(2,1)S(1)}, bf16[512,2304]{1,0:T(8,128)(2,1)}, s32[]{:T(128)}) %tuple.130), branch_computations={%region_4.5_spmd, %region_5.6_spmd} | conditional | flops 604798976 | bytes 12321226 | solution.py:39
  48.4 371.5 %while.17 = (s32[]{:T(128)}, f32[16,2048]{1,0:T(8,128)}, s32[]{:T(128)}, s32[16]{0:T(128)S(1)}, bf16[8,256,512]{2,1,0:T(8,128)(2,1)}, /*index=5*/bf16[512,2304]{...) while((s32[]{:T(128)}, f32[16,2048]{1,0:T(8,128)}, ...), condition=%wide.region_3.4_spmd, body=%wide.region_0.3_spmd.sunk | while | flops 604831744 | bytes 13763416 | solution.py:99
  49.6 14.7 %conditional.4 = (f32[16,2048]{1,0:T(8,128)}) conditional(s32[]{:T(128)} %convert_element_type.41, () %tuple.111, (s32[]{:T(128)}, bf16[8,256,512]{2,1,0:T(8,128)(2,1)}, bf16[512,2304]{1,0:T(8,128)(2,1)S(1)}, bf16[512,2304]{1,0:T(8,128)(2,1)}, s32[]{:T(128)}) %tuple.112), branch_computations={%region_1.1_spmd, %region_2.2_spmd} | conditional | flops 604798976 | bytes 12321226 | solution.py:39
  65.4 7.2 %collective-permute-done = f32[16,2048]{1,0:T(8,128)S(1)} collective-permute-done((f32[16,2048]{1,0:T(8,128)S(1)}, f32[16,2048]{1,0:T(8,128)S(1)}, u32[]{:S(2)}, u32[]{:S(2)}) %collective-permute-start) | collective-permute-done | bytes 131104 | tf_op jit(solution)/shard_map/while/body/eval_jaxpr/ppermute | solution.py:18
  74.5 14.7 %conditional.4 = (f32[16,2048]{1,0:T(8,128)}) conditional(s32[]{:T(128)} %convert_element_type.41, () %tuple.111, (s32[]{:T(128)}, bf16[8,256,512]{2,1,0:T(8,128)(2,1)}, bf16[512,2304]{1,0:T(8,128)(2,1)S(1)}, bf16[512,2304]{1,0:T(8,128)(2,1)}, s32[]{:T(128)}) %tuple.112), branch_computations={%region_1.1_spmd, %region_2.2_spmd} | conditional | flops 604798976 | bytes 12321226 | solution.py:39
  99.3 14.7 %conditional.4 = (f32[16,2048]{1,0:T(8,128)}) conditional(s32[]{:T(128)} %convert_element_type.41, () %tuple.111, (s32[]{:T(128)}, bf16[8,256,512]{2,1,0:T(8,128)(2,1)}, bf16[512,2304]{1,0:T(8,128)(2,1)S(1)}, bf16[512,2304]{1,0:T(8,128)(2,1)}, s32[]{:T(128)}) %tuple.112), branch_computations={%region_1.1_spmd, %region_2.2_spmd} | conditional | flops 604798976 | bytes 12321226 | solution.py:39
  115.1 7.1 %collective-permute-done = f32[16,2048]{1,0:T(8,128)S(1)} collective-permute-done((f32[16,2048]{1,0:T(8,128)S(1)}, f32[16,2048]{1,0:T(8,128)S(1)}, u32[]{:S(2)}, u32[]{:S(2)}) %collective-permute-start) | collective-permute-done | bytes 131104 | tf_op jit(solution)/shard_map/while/body/eval_jaxpr/ppermute | solution.py:18
  124.0 14.7 %conditional.4 = (f32[16,2048]{1,0:T(8,128)}) conditional(s32[]{:T(128)} %convert_element_type.41, () %tuple.111, (s32[]{:T(128)}, bf16[8,256,512]{2,1,0:T(8,128)(2,1)}, bf16[512,2304]{1,0:T(8,128)(2,1)S(1)}, bf16[512,2304]{1,0:T(8,128)(2,1)}, s32[]{:T(128)}) %tuple.112), branch_computations={%region_1.1_spmd, %region_2.2_spmd} | conditional | flops 604798976 | bytes 12321226 | solution.py:39
  139.8 7.1 %collective-permute-done = f32[16,2048]{1,0:T(8,128)S(1)} collective-permute-done((f32[16,2048]{1,0:T(8,128)S(1)}, f32[16,2048]{1,0:T(8,128)S(1)}, u32[]{:S(2)}, u32[]{:S(2)}) %collective-permute-start) | collective-permute-done | bytes 131104 | tf_op jit(solution)/shard_map/while/body/eval_jaxpr/ppermute | solution.py:18
  148.8 14.7 %conditional.4 = (f32[16,2048]{1,0:T(8,128)}) conditional(s32[]{:T(128)} %convert_element_type.41, () %tuple.111, (s32[]{:T(128)}, bf16[8,256,512]{2,1,0:T(8,128)(2,1)}, bf16[512,2304]{1,0:T(8,128)(2,1)S(1)}, bf16[512,2304]{1,0:T(8,128)(2,1)}, s32[]{:T(128)}) %tuple.112), branch_computations={%region_1.1_spmd, %region_2.2_spmd} | conditional | flops 604798976 | bytes 12321226 | solution.py:39
  173.5 14.7 %conditional.4 = (f32[16,2048]{1,0:T(8,128)}) conditional(s32[]{:T(128)} %convert_element_type.41, () %tuple.111, (s32[]{:T(128)}, bf16[8,256,512]{2,1,0:T(8,128)(2,1)}, bf16[512,2304]{1,0:T(8,128)(2,1)S(1)}, bf16[512,2304]{1,0:T(8,128)(2,1)}, s32[]{:T(128)}) %tuple.112), branch_computations={%region_1.1_spmd, %region_2.2_spmd} | conditional | flops 604798976 | bytes 12321226 | solution.py:39
  198.3 14.7 %conditional.4 = (f32[16,2048]{1,0:T(8,128)}) conditional(s32[]{:T(128)} %convert_element_type.41, () %tuple.111, (s32[]{:T(128)}, bf16[8,256,512]{2,1,0:T(8,128)(2,1)}, bf16[512,2304]{1,0:T(8,128)(2,1)S(1)}, bf16[512,2304]{1,0:T(8,128)(2,1)}, s32[]{:T(128)}) %tuple.112), branch_computations={%region_1.1_spmd, %region_2.2_spmd} | conditional | flops 604798976 | bytes 12321226 | solution.py:39
  223.1 14.7 %conditional.4 = (f32[16,2048]{1,0:T(8,128)}) conditional(s32[]{:T(128)} %convert_element_type.41, () %tuple.111, (s32[]{:T(128)}, bf16[8,256,512]{2,1,0:T(8,128)(2,1)}, bf16[512,2304]{1,0:T(8,128)(2,1)S(1)}, bf16[512,2304]{1,0:T(8,128)(2,1)}, s32[]{:T(128)}) %tuple.112), branch_computations={%region_1.1_spmd, %region_2.2_spmd} | conditional | flops 604798976 | bytes 12321226 | solution.py:39
  247.8 14.7 %conditional.4 = (f32[16,2048]{1,0:T(8,128)}) conditional(s32[]{:T(128)} %convert_element_type.41, () %tuple.111, (s32[]{:T(128)}, bf16[8,256,512]{2,1,0:T(8,128)(2,1)}, bf16[512,2304]{1,0:T(8,128)(2,1)S(1)}, bf16[512,2304]{1,0:T(8,128)(2,1)}, s32[]{:T(128)}) %tuple.112), branch_computations={%region_1.1_spmd, %region_2.2_spmd} | conditional | flops 604798976 | bytes 12321226 | solution.py:39
  272.6 14.7 %conditional.4 = (f32[16,2048]{1,0:T(8,128)}) conditional(s32[]{:T(128)} %convert_element_type.41, () %tuple.111, (s32[]{:T(128)}, bf16[8,256,512]{2,1,0:T(8,128)(2,1)}, bf16[512,2304]{1,0:T(8,128)(2,1)S(1)}, bf16[512,2304]{1,0:T(8,128)(2,1)}, s32[]{:T(128)}) %tuple.112), branch_computations={%region_1.1_spmd, %region_2.2_spmd} | conditional | flops 604798976 | bytes 12321226 | solution.py:39
  297.3 14.7 %conditional.4 = (f32[16,2048]{1,0:T(8,128)}) conditional(s32[]{:T(128)} %convert_element_type.41, () %tuple.111, (s32[]{:T(128)}, bf16[8,256,512]{2,1,0:T(8,128)(2,1)}, bf16[512,2304]{1,0:T(8,128)(2,1)S(1)}, bf16[512,2304]{1,0:T(8,128)(2,1)}, s32[]{:T(128)}) %tuple.112), branch_computations={%region_1.1_spmd, %region_2.2_spmd} | conditional | flops 604798976 | bytes 12321226 | solution.py:39
  322.1 14.7 %conditional.4 = (f32[16,2048]{1,0:T(8,128)}) conditional(s32[]{:T(128)} %convert_element_type.41, () %tuple.111, (s32[]{:T(128)}, bf16[8,256,512]{2,1,0:T(8,128)(2,1)}, bf16[512,2304]{1,0:T(8,128)(2,1)S(1)}, bf16[512,2304]{1,0:T(8,128)(2,1)}, s32[]{:T(128)}) %tuple.112), branch_computations={%region_1.1_spmd, %region_2.2_spmd} | conditional | flops 604798976 | bytes 12321226 | solution.py:39
  346.9 14.7 %conditional.4 = (f32[16,2048]{1,0:T(8,128)}) conditional(s32[]{:T(128)} %convert_element_type.41, () %tuple.111, (s32[]{:T(128)}, bf16[8,256,512]{2,1,0:T(8,128)(2,1)}, bf16[512,2304]{1,0:T(8,128)(2,1)S(1)}, bf16[512,2304]{1,0:T(8,128)(2,1)}, s32[]{:T(128)}) %tuple.112), branch_computations={%region_1.1_spmd, %region_2.2_spmd} | conditional | flops 604798976 | bytes 12321226 | solution.py:39
  371.6 14.7 %conditional.4 = (f32[16,2048]{1,0:T(8,128)}) conditional(s32[]{:T(128)} %convert_element_type.41, () %tuple.111, (s32[]{:T(128)}, bf16[8,256,512]{2,1,0:T(8,128)(2,1)}, bf16[512,2304]{1,0:T(8,128)(2,1)S(1)}, bf16[512,2304]{1,0:T(8,128)(2,1)}, s32[]{:T(128)}) %tuple.112), branch_computations={%region_1.1_spmd, %region_2.2_spmd} | conditional | flops 604798976 | bytes 12321226 | solution.py:39
  396.4 14.7 %conditional.4 = (f32[16,2048]{1,0:T(8,128)}) conditional(s32[]{:T(128)} %convert_element_type.41, () %tuple.111, (s32[]{:T(128)}, bf16[8,256,512]{2,1,0:T(8,128)(2,1)}, bf16[512,2304]{1,0:T(8,128)(2,1)S(1)}, bf16[512,2304]{1,0:T(8,128)(2,1)}, s32[]{:T(128)}) %tuple.112), branch_computations={%region_1.1_spmd, %region_2.2_spmd} | conditional | flops 604798976 | bytes 12321226 | solution.py:39
  420.9 33.7 %while.19 = (s32[]{:T(128)}, f32[16,2048]{1,0:T(8,128)S(1)}, s32[16,2]{0,1:T(2,128)S(1)}, f32[16,1024]{1,0:T(8,128)S(1)}, s32[]{:T(128)}, /*index=5*/s32[]{:T(128)}) while((s32[]{:T(128)}, f32[16,2048]{1,0:T(8,128)S(1)}, s32[16,2]{0,1:T(2,128)S(1)}, f32[16,1024]{1,0:T(8,128)S(1)}, s32[]{:T(128)}, /*index=5*/s32[]{:T(128)}) %tuple.120), condition=%wide.while_cond.1, body=%wide.while_body.1.sunk | while | flops 2 | bytes 16505 | solution.py:59
  454.7 33.7 %while.18 = (s32[]{:T(128)}, f32[16,2048]{1,0:T(8,128)S(1)}, s32[16,2]{0,1:T(2,128)S(1)}, f32[16,1024]{1,0:T(8,128)S(1)}, s32[]{:T(128)}, /*index=5*/s32[]{:T(128)}) while((s32[]{:T(128)}, f32[16,2048]{1,0:T(8,128)S(1)}, s32[16,2]{0,1:T(2,128)S(1)}, f32[16,1024]{1,0:T(8,128)S(1)}, s32[]{:T(128)}, /*index=5*/s32[]{:T(128)}) %tuple.132), condition=%wide.while_cond, body=%wide.while_body.sunk | while | flops 2 | bytes 16505 | solution.py:59
  (323 shorter events, 279.5 us)
Async XLA Ops:
  0.6 32.2 %collective-permute-start.1 = (bf16[4,1,128,2304]{3,2,1,0:T(8,128)(2,1)}, bf16[4,1,128,2304]{3,2,1,0:T(8,128)(2,1)}, u32[]{:S(2)}, u32[]{:S(2)}) collective-permute-start(bf16[4,1,128,2304]{3,2,1,0:T(8,128)(2,1)} %param.10), channel_id=1, source_target_pairs={{1,0},{2,1},{3,2},{4,3},{5,4},{6,5},{7,6},{8,7},{9,8},{10,9},{11,1... | collective-permute-start | bytes 7077896 | tf_op jit(solution)/shard_map/ppermute | solution.py:18
  6.1 4.2 copy-start.4
  6.1 6.1 %copy-start.3 = (s32[16]{0:T(128)S(1)}, s32[16]{0:T(128)}, u32[]{:S(2)}) copy-start(s32[16]{0:T(128)} %param.13) | copy-start | bytes 196
  12.3 20.5 %copy-start = (bf16[4,1,128,2304]{3,2,1,0:T(8,128)(2,1)S(1)}, bf16[4,1,128,2304]{3,2,1,0:T(8,128)(2,1)}, u32[]{:S(2)}) copy-start(bf16[4,1,128,2304]{3,2,1,0:T(8,128)(2,1)} %param.10) | copy-start | bytes 7077892
  65.3 7.3 %collective-permute-start = (f32[16,2048]{1,0:T(8,128)S(1)}, f32[16,2048]{1,0:T(8,128)S(1)}, u32[]{:S(2)}, u32[]{:S(2)}) collective-permute-start(f32[16,2048]{1,0:T(8,128)S(1)} %add.404), channel_id=1, source_target_pairs={{15,0},{0,1},{1,2},{2,3},{3,4},{4,5},{5,6},{6,7},{7,8},{8,9},{9,10... | collective-permute-start | bytes 393224 | tf_op jit(solution)/shard_map/while/body/eval_jaxpr/ppermute | solution.py:18
  72.6 0.7 copy-start.1
  90.2 7.1 %collective-permute-start = (f32[16,2048]{1,0:T(8,128)S(1)}, f32[16,2048]{1,0:T(8,128)S(1)}, u32[]{:S(2)}, u32[]{:S(2)}) collective-permute-start(f32[16,2048]{1,0:T(8,128)S(1)} %add.404), channel_id=1, source_target_pairs={{15,0},{0,1},{1,2},{2,3},{3,4},{4,5},{5,6},{6,7},{7,8},{8,9},{9,10... | collective-permute-start | bytes 393224 | tf_op jit(solution)/shard_map/while/body/eval_jaxpr/ppermute | solution.py:18
  97.4 0.7 copy-start.1
  115.0 7.1 %collective-permute-start = (f32[16,2048]{1,0:T(8,128)S(1)}, f32[16,2048]{1,0:T(8,128)S(1)}, u32[]{:S(2)}, u32[]{:S(2)}) collective-permute-start(f32[16,2048]{1,0:T(8,128)S(1)} %add.404), channel_id=1, source_target_pairs={{15,0},{0,1},{1,2},{2,3},{3,4},{4,5},{5,6},{6,7},{7,8},{8,9},{9,10... | collective-permute-start | bytes 393224 | tf_op jit(solution)/shard_map/while/body/eval_jaxpr/ppermute | solution.py:18
  122.1 0.7 copy-start.1
  139.8 7.1 %collective-permute-start = (f32[16,2048]{1,0:T(8,128)S(1)}, f32[16,2048]{1,0:T(8,128)S(1)}, u32[]{:S(2)}, u32[]{:S(2)}) collective-permute-start(f32[16,2048]{1,0:T(8,128)S(1)} %add.404), channel_id=1, source_target_pairs={{15,0},{0,1},{1,2},{2,3},{3,4},{4,5},{5,6},{6,7},{7,8},{8,9},{9,10... | collective-permute-start | bytes 393224 | tf_op jit(solution)/shard_map/while/body/eval_jaxpr/ppermute | solution.py:18
  146.9 0.7 copy-start.1
  164.5 7.1 %collective-permute-start = (f32[16,2048]{1,0:T(8,128)S(1)}, f32[16,2048]{1,0:T(8,128)S(1)}, u32[]{:S(2)}, u32[]{:S(2)}) collective-permute-start(f32[16,2048]{1,0:T(8,128)S(1)} %add.404), channel_id=1, source_target_pairs={{15,0},{0,1},{1,2},{2,3},{3,4},{4,5},{5,6},{6,7},{7,8},{8,9},{9,10... | collective-permute-start | bytes 393224 | tf_op jit(solution)/shard_map/while/body/eval_jaxpr/ppermute | solution.py:18
  189.3 7.1 %collective-permute-start = (f32[16,2048]{1,0:T(8,128)S(1)}, f32[16,2048]{1,0:T(8,128)S(1)}, u32[]{:S(2)}, u32[]{:S(2)}) collective-permute-start(f32[16,2048]{1,0:T(8,128)S(1)} %add.404), channel_id=1, source_target_pairs={{15,0},{0,1},{1,2},{2,3},{3,4},{4,5},{5,6},{6,7},{7,8},{8,9},{9,10... | collective-permute-start | bytes 393224 | tf_op jit(solution)/shard_map/while/body/eval_jaxpr/ppermute | solution.py:18
  214.0 7.1 %collective-permute-start = (f32[16,2048]{1,0:T(8,128)S(1)}, f32[16,2048]{1,0:T(8,128)S(1)}, u32[]{:S(2)}, u32[]{:S(2)}) collective-permute-start(f32[16,2048]{1,0:T(8,128)S(1)} %add.404), channel_id=1, source_target_pairs={{15,0},{0,1},{1,2},{2,3},{3,4},{4,5},{5,6},{6,7},{7,8},{8,9},{9,10... | collective-permute-start | bytes 393224 | tf_op jit(solution)/shard_map/while/body/eval_jaxpr/ppermute | solution.py:18
  238.8 7.1 %collective-permute-start = (f32[16,2048]{1,0:T(8,128)S(1)}, f32[16,2048]{1,0:T(8,128)S(1)}, u32[]{:S(2)}, u32[]{:S(2)}) collective-permute-start(f32[16,2048]{1,0:T(8,128)S(1)} %add.404), channel_id=1, source_target_pairs={{15,0},{0,1},{1,2},{2,3},{3,4},{4,5},{5,6},{6,7},{7,8},{8,9},{9,10... | collective-permute-start | bytes 393224 | tf_op jit(solution)/shard_map/while/body/eval_jaxpr/ppermute | solution.py:18
  263.6 7.1 %collective-permute-start = (f32[16,2048]{1,0:T(8,128)S(1)}, f32[16,2048]{1,0:T(8,128)S(1)}, u32[]{:S(2)}, u32[]{:S(2)}) collective-permute-start(f32[16,2048]{1,0:T(8,128)S(1)} %add.404), channel_id=1, source_target_pairs={{15,0},{0,1},{1,2},{2,3},{3,4},{4,5},{5,6},{6,7},{7,8},{8,9},{9,10... | collective-permute-start | bytes 393224 | tf_op jit(solution)/shard_map/while/body/eval_jaxpr/ppermute | solution.py:18
  288.3 7.1 %collective-permute-start = (f32[16,2048]{1,0:T(8,128)S(1)}, f32[16,2048]{1,0:T(8,128)S(1)}, u32[]{:S(2)}, u32[]{:S(2)}) collective-permute-start(f32[16,2048]{1,0:T(8,128)S(1)} %add.404), channel_id=1, source_target_pairs={{15,0},{0,1},{1,2},{2,3},{3,4},{4,5},{5,6},{6,7},{7,8},{8,9},{9,10... | collective-permute-start | bytes 393224 | tf_op jit(solution)/shard_map/while/body/eval_jaxpr/ppermute | solution.py:18
  313.1 7.1 %collective-permute-start = (f32[16,2048]{1,0:T(8,128)S(1)}, f32[16,2048]{1,0:T(8,128)S(1)}, u32[]{:S(2)}, u32[]{:S(2)}) collective-permute-start(f32[16,2048]{1,0:T(8,128)S(1)} %add.404), channel_id=1, source_target_pairs={{15,0},{0,1},{1,2},{2,3},{3,4},{4,5},{5,6},{6,7},{7,8},{8,9},{9,10... | collective-permute-start | bytes 393224 | tf_op jit(solution)/shard_map/while/body/eval_jaxpr/ppermute | solution.py:18
  337.8 7.1 %collective-permute-start = (f32[16,2048]{1,0:T(8,128)S(1)}, f32[16,2048]{1,0:T(8,128)S(1)}, u32[]{:S(2)}, u32[]{:S(2)}) collective-permute-start(f32[16,2048]{1,0:T(8,128)S(1)} %add.404), channel_id=1, source_target_pairs={{15,0},{0,1},{1,2},{2,3},{3,4},{4,5},{5,6},{6,7},{7,8},{8,9},{9,10... | collective-permute-start | bytes 393224 | tf_op jit(solution)/shard_map/while/body/eval_jaxpr/ppermute | solution.py:18
  362.6 7.1 %collective-permute-start = (f32[16,2048]{1,0:T(8,128)S(1)}, f32[16,2048]{1,0:T(8,128)S(1)}, u32[]{:S(2)}, u32[]{:S(2)}) collective-permute-start(f32[16,2048]{1,0:T(8,128)S(1)} %add.404), channel_id=1, source_target_pairs={{15,0},{0,1},{1,2},{2,3},{3,4},{4,5},{5,6},{6,7},{7,8},{8,9},{9,10... | collective-permute-start | bytes 393224 | tf_op jit(solution)/shard_map/while/body/eval_jaxpr/ppermute | solution.py:18
  387.3 7.1 %collective-permute-start = (f32[16,2048]{1,0:T(8,128)S(1)}, f32[16,2048]{1,0:T(8,128)S(1)}, u32[]{:S(2)}, u32[]{:S(2)}) collective-permute-start(f32[16,2048]{1,0:T(8,128)S(1)} %add.404), channel_id=1, source_target_pairs={{15,0},{0,1},{1,2},{2,3},{3,4},{4,5},{5,6},{6,7},{7,8},{8,9},{9,10... | collective-permute-start | bytes 393224 | tf_op jit(solution)/shard_map/while/body/eval_jaxpr/ppermute | solution.py:18
  412.1 7.1 %collective-permute-start = (f32[16,2048]{1,0:T(8,128)S(1)}, f32[16,2048]{1,0:T(8,128)S(1)}, u32[]{:S(2)}, u32[]{:S(2)}) collective-permute-start(f32[16,2048]{1,0:T(8,128)S(1)} %add.404), channel_id=1, source_target_pairs={{15,0},{0,1},{1,2},{2,3},{3,4},{4,5},{5,6},{6,7},{7,8},{8,9},{9,10... | collective-permute-start | bytes 393224 | tf_op jit(solution)/shard_map/while/body/eval_jaxpr/ppermute | solution.py:18
  488.4 5.1 %copy-start.2 = (f32[16,2048]{1,0:T(8,128)}, f32[16,2048]{1,0:T(8,128)S(1)}, u32[]{:S(2)}) copy-start(f32[16,2048]{1,0:T(8,128)S(1)} %get-tuple-element.560) | copy-start | bytes 393220
  (11 other events, 7.2 us)
where the time goes:
time: 499 us; the launch traced here: 495 us
  loops' own time  172 us (34%)
  waiting for transfers between devices  118 us (24%)
  local copies, waits for them, and re-layouts  107 us (21%)
  matrix products  47.1 us (9%)
  other arithmetic  43.2 us (9%)
  starting transfers between devices  6.37 us (1%)
    another operation x16, loops' own time, pair_term(): return lax.cond(offset >= 0, compute, skipped)  162 us
    ppermute x16, waiting for transfers between devices, shifted(): return lax.ppermute(block, axis, route)  118 us
    gather x128, local copies, waits for them, and re-layouts  66.7 us
    dot_general x32, matrix products, compute(): jnp.dot(amp_rows, node_rows, preferred_element_type=jnp.float32)  42.2 us
    add x16, other arithmetic, compute(): summed + lax.dynamic_slice_in_dim(delayed[tap_index], HEAD - offset - tap...  16.3 us
    dynamic_slice x16, local copies, waits for them, and re-layouts, observer_term(): lax.dynamic_slice_in_dim(amp_table, obs_block * observers, observers, axi...  14.8 us
    add x15, other arithmetic, advance(): return shifted(carried + observer_term(obs_block, NSAMP), 'az', 1)  14.7 us
  transfers between devices with their start and end apart: 16, of which 16 were waited for; matrix products, arithmetic and copies ran while one was open for 3% of the time, Pallas kernels for 0%

commit v1 on v0

--- a/solution.py
+++ b/solution.py
@@ -1,6 +1,12 @@
+import functools
+
 import jax
 import jax.numpy as jnp
+import ml_dtypes
+import numpy as np
 from jax import lax
+from jax.experimental import pallas as pl
+from jax.experimental.pallas import tpu as pltpu
 from jax.sharding import PartitionSpec as P
 
 NAXIAL = 128
@@ -73,7 +79,7 @@
     return jnp.mean(power.reshape(num_rows, NSEG, half_seg), axis=1) / energy
 
 
-def on_device(surface_nodes, amplitudes, block_offsets, welch_first):
+def general_device(surface_nodes, amplitudes, block_offsets, welch_first):
     cycle_size = lax.axis_size("az")
     position = lax.axis_index("az")
     observers = NO // cycle_size
@@ -102,6 +108,224 @@
     return (pressure, spectra)
 
 
+NSRC = NSAMP + HEAD
+CHUNK = 256
+N_IN = NSRC // CHUNK
+N_OUT = NSAMP // CHUNK
+NZ = 4
+OBS = 16
+MESH = pl.DeviceIdType.MESH
+
+
+def basis_parts():
+    n = np.arange(SEG)
+    f = np.arange(SEG // 2)
+    angles = 2.0 * np.pi / SEG * ((n[:, None] * f[None, :]) % SEG)
+    window = 0.5 - 0.5 * np.cos(2.0 * np.pi / SEG * n)
+    basis = np.concatenate([np.cos(angles), -np.sin(angles)], axis=1) * window[:, None]
+    high = basis.astype(np.float32).astype(ml_dtypes.bfloat16)
+    low = (basis - high.astype(np.float64)).astype(np.float32).astype(ml_dtypes.bfloat16)
+    return np.stack([high, low]), float(np.sum(window * window))
+
+
+def moved(part, distance, levels, width):
+    for level in range(levels - 1, 6, -1):
+        step = 1 << level
+        size = part.shape[1] - (step if step < 1 << (levels - 1) else 0)
+        chosen = (distance[:, :size] & step) != 0
+        if size == part.shape[1]:
+            ahead = jnp.concatenate([part[:, step:], part[:, :step]], axis=1)
+        else:
+            ahead = part[:, step:]
+        part = jnp.where(chosen, ahead, part[:, :size])
+    size = part.shape[1]
+    for level in range(7):
+        step = 1 << level
+        part = jnp.where((distance[:, :size] & step) != 0, pltpu.roll(part, size - step, axis=1), part)
+    return part[:, :width]
+
+
+def fused(
+    energy,
+    offs, first, nodes, amps, basis_hbm,
+    pressure_out, spectra_out,
+    own, following, basis, carry, series, terms, got_core, got_y, got_z, padded,
+    x_send, x_recv, c_send, c_recv, y_send, y_recv, z_send, z_recv, local_sem,
+):
+    me = lax.axis_index("az")
+    core = lax.rem(me, 2)
+    y = lax.rem(me // 2, 2)
+    z = me // 4
+    left = lax.rem(me + 15, 16)
+    right = lax.rem(me + 1, 16)
+    sibling = z * 4 + y * 2 + (1 - core)
+    across = z * 4 + (1 - y) * 2 + core
+
+    def along(r):
+        return lax.rem(z + r, NZ) * 4 + y * 2 + core
+
+    own_copy = pltpu.make_async_copy(nodes, own, local_sem.at[0])
+    own_copy.start()
+    basis_copy = pltpu.make_async_copy(basis_hbm, basis, local_sem.at[1])
+    basis_copy.start()
+
+    barrier = pltpu.get_barrier_semaphore()
+    for partner in (left, right, across, along(1), along(2), along(3)):
+        pl.semaphore_signal(barrier, inc=1, device_id={"az": partner}, device_id_type=MESH)
+    pl.semaphore_wait(barrier, 6)
+
+    def remote(src, dst, send, recv, target):
+        return pltpu.make_async_remote_copy(
+            src_ref=src, dst_ref=dst, send_sem=send, recv_sem=recv,
+            device_id={"az": target}, device_id_type=MESH,
+        )
+
+    x_copies = []
+    for j in range(N_IN):
+        cols = pl.ds(j * CHUNK, CHUNK)
+        x_copies.append(remote(nodes.at[:, :, cols], following.at[:, :, cols], x_send.at[j], x_recv.at[j], left))
+        x_copies[-1].start()
+
+    carry[...] = jnp.zeros_like(carry)
+    lane0 = lax.broadcasted_iota(jnp.int32, (32, 128), 1) == 0
+    own_copy.wait()
+
+    def delayed(j):
+        cols = pl.ds(j * CHUNK, CHUNK)
+
+        def body(pair, _):
+            rows = pl.ds(pl.multiple_of(pair * 32, 32), 32)
+            a = amps[:, rows, :].reshape(KTAPS * 32, 4 * NAXIAL)
+            d = jnp.dot(a, own[:, :, cols].reshape(4 * NAXIAL, CHUNK), preferred_element_type=jnp.float32)
+            d = d + jnp.dot(a, following[:, :, cols].reshape(4 * NAXIAL, CHUNK), preferred_element_type=jnp.float32)
+            d = d.reshape(KTAPS, 32, CHUNK)
+            total = d[KTAPS - 1]
+            for m in range(KTAPS - 2, -1, -1):
+                turned = pltpu.roll(total, 1, axis=1)
+                before = carry[m, rows, :]
+                carry[m, rows, :] = turned[:, :128]
+                lead = jnp.where(lane0, before, turned[:, :128])
+                total = d[m] + jnp.concatenate([lead, turned[:, 128:]], axis=1)
+            series[rows, cols] = 0.5 * total
+            return 0
+
+        lax.fori_loop(0, NO // 32, body, 0)
+
+    def make_terms(q):
+        def body(b, _):
+            offset = offs[0, b]
+            shift = HEAD - jnp.maximum(offset, 0)
+            rows = pl.ds(pl.multiple_of(b * OBS, OBS), OBS)
+            part = series[rows, pl.ds(q * CHUNK, CHUNK + HEAD)]
+            part = moved(part, jnp.full((OBS, CHUNK + HEAD), shift, jnp.int32), 9, CHUNK)
+            part = jnp.where(jnp.full((OBS, CHUNK), offset, jnp.int32) >= 0, part, 0.0)
+            terms[q, lax.rem(b, 2), lax.rem(b // 2, 2), b // 4] = part
+            return 0
+
+        lax.fori_loop(0, 16, body, 0)
+
+    c_copies, y_copies, z_copies = [], [], []
+    for j in range(N_IN + 4):
+        if j < N_IN:
+            x_copies[j].wait_recv()
+            delayed(j)
+        q = j - 1
+        if 0 <= q < N_OUT:
+            make_terms(q)
+            c_copies.append(remote(terms.at[q, 1 - core], got_core.at[q], c_send.at[q], c_recv.at[q], sibling))
+            c_copies[q].start()
+        q = j - 2
+        if 0 <= q < N_OUT:
+            c_copies[q].wait_recv()
+            terms[q, core] = terms[q, core] + got_core[q]
+            y_copies.append(remote(terms.at[q, core, 1 - y], got_y.at[q], y_send.at[q], y_recv.at[q], across))
+            y_copies[q].start()
+        q = j - 3
+        if 0 <= q < N_OUT:
+            y_copies[q].wait_recv()
+            terms[q, core, y] = terms[q, core, y] + got_y[q]
+            z_copies.append([])
+            for r in range(1, NZ):
+                z_copies[q].append(
+                    remote(terms.at[q, core, y, lax.rem(z + r, NZ)], got_z.at[q, r - 1], z_send.at[q, r - 1], z_recv.at[q, r - 1], along(r))
+                )
+                z_copies[q][-1].start()
+        q = j - 4
+        if 0 <= q < N_OUT:
+            result = terms[q, core, y, z]
+            for r in range(1, NZ):
+                z_copies[q][r - 1].wait_recv()
+                result = result + got_z[q, r - 1]
+            cols = pl.ds(q * CHUNK, CHUNK)
+            padded[:, cols] = result
+            pressure_out[:, cols] = result
+
+    width = SEG + SEG // 2
+
+    row_ids = lax.broadcasted_iota(jnp.int32, (OBS, NSAMP), 0)
+    distance = jnp.zeros((OBS, NSAMP), jnp.int32)
+    for o in range(OBS):
+        distance = jnp.where(row_ids == o, first[o], distance)
+    segments = moved(padded[...], distance, 10, width)
+    basis_copy.wait()
+    both = jnp.concatenate([segments[:, :SEG], segments[:, SEG // 2 : width]], axis=0)
+    high = both.astype(jnp.bfloat16)
+    low = (both - high.astype(jnp.float32)).astype(jnp.bfloat16)
+    stacked = jnp.concatenate([high, low], axis=0)
+    for f in range(0, SEG // 2, CHUNK):
+        power = None
+        for base in (0, SEG // 2):
+            cols = pl.ds(base + f, CHUNK)
+            main = jnp.dot(stacked, basis[0, :, cols], preferred_element_type=jnp.float32)
+            rest = jnp.dot(high, basis[1, :, cols], preferred_element_type=jnp.float32)
+            coeffs = main[: 2 * OBS] + main[2 * OBS :] + rest
+            power = coeffs * coeffs if power is None else power + coeffs * coeffs
+        spectra_out[:, pl.ds(f, CHUNK)] = (power[:OBS] + power[OBS:]) * (0.5 / energy)
+
+    for copy in x_copies + c_copies + y_copies + sum(z_copies, []):
+        copy.wait_send()
+
+
+def fast_device(surface_nodes, amplitudes, block_offsets, welch_first):
+    basis, energy = basis_parts()
+    nodes = surface_nodes.reshape(4, NAXIAL, NSRC)
+    amps = amplitudes.reshape(KTAPS, NO, 4 * NAXIAL)
+    vmem = pl.BlockSpec(memory_space=pltpu.VMEM)
+    smem = pl.BlockSpec(memory_space=pltpu.SMEM)
+    anywhere = pl.BlockSpec(memory_space=pl.ANY)
+    dma = pltpu.SemaphoreType.DMA
+    f32 = jnp.float32
+    return pl.pallas_call(
+        functools.partial(fused, energy),
+        out_shape=(
+            jax.ShapeDtypeStruct((OBS, NSAMP), f32),
+            jax.ShapeDtypeStruct((OBS, SEG // 2), f32),
+        ),
+        in_specs=[smem, smem, anywhere, vmem, anywhere],
+        out_specs=(vmem, vmem),
+        scratch_shapes=[
+            pltpu.VMEM((4, NAXIAL, NSRC), jnp.bfloat16),
+            pltpu.VMEM((4, NAXIAL, NSRC), jnp.bfloat16),
+            pltpu.VMEM((2, SEG, SEG), jnp.bfloat16),
+            pltpu.VMEM((KTAPS - 1, NO, 128), f32),
+            pltpu.VMEM((NO, NSRC), f32),
+            pltpu.VMEM((N_OUT, 2, 2, NZ, OBS, CHUNK), f32),
+            pltpu.VMEM((N_OUT, 2, NZ, OBS, CHUNK), f32),
+            pltpu.VMEM((N_OUT, NZ, OBS, CHUNK), f32),
+            pltpu.VMEM((N_OUT, NZ - 1, OBS, CHUNK), f32),
+            pltpu.VMEM((OBS, NSAMP), f32),
+            dma((N_IN,)), dma((N_IN,)),
+            dma((N_OUT,)), dma((N_OUT,)),
+            dma((N_OUT,)), dma((N_OUT,)),
+            dma((N_OUT, NZ - 1)), dma((N_OUT, NZ - 1)),
+            dma((2,)),
+        ],
+        compiler_params=pltpu.CompilerParams(
+            collective_id=0, has_side_effects=True, vmem_limit_bytes=44 * 1024 * 1024
+        ),
+    )(block_offsets, welch_first, nodes, amps, jnp.asarray(basis))
+
+
 def solution(mesh):
     placed = (
         P("groups", "az", None, None),
@@ -110,7 +334,7 @@
         P(("groups", "az")),
     )
     return jax.shard_map(
-        on_device,
+        fast_device if mesh.shape["az"] == 16 else general_device,
         mesh=mesh,
         in_specs=placed,
         out_specs=(P(("groups", "az"), None), P(("groups", "az"), None)),

time: 499 us -> 154 us (0.31)
  loops' own time: 172 us -> 0 us
  Pallas kernels: 0 us -> 146 us
  waiting for transfers between devices: 118 us -> 0 us
  local copies, waits for them, and re-layouts: 107 us -> 7.89 us
  matrix products: 47.1 us -> 0 us
  other arithmetic: 43.2 us -> 0 us
  starting transfers between devices: 6.37 us -> 0 us
    another operation x19 -> x0, loops' own time: 172 us -> none  [the longest x16 162 us: pair_term(): return lax.cond(offset >= 0, compute, skipped)]
    pallas_call x0 -> x1, Pallas kernels: none -> 146 us  [fast_device(): pl.pallas_call(functools.partial(fused, energy), out_shape=(jax.ShapeDtyp...]
    ppermute x16 -> x0, waiting for transfers between devices: 118 us -> none  [shifted(): return lax.ppermute(block, axis, route)]
    gather x128 -> x0, local copies, waits for them, and re-layouts: 66.7 us -> none
    dot_general x33 -> x0, matrix products: 47.1 us -> none  [the longest x32 42.2 us: compute(): jnp.dot(amp_rows, node_rows, preferred_element_type=jnp.float32)]
    add x33 -> x0, other arithmetic: 32 us -> none  [the longest x16 16.3 us: compute(): summed + lax.dynamic_slice_in_dim(delayed[tap_index], HEAD - offset - tap...]
    dynamic_slice x32 -> x0, local copies, waits for them, and re-layouts: 24.3 us -> none  [the longest x16 14.8 us: observer_term(): lax.dynamic_slice_in_dim(amp_table, obs_block * observers, observers, axi...]
    while x30 -> x0, local copies, waits for them, and re-layouts: 9.82 us -> none
  transfers between devices with their start and end apart: 16 -> 0, of which waited for: 16 -> 0; matrix products, arithmetic and copies ran while one was open for 3% -> 0% of each run, Pallas kernels for 0% -> 0%
where the time goes in v1:
time: 154 us
  Pallas kernels  146 us (95%)
  local copies, waits for them, and re-layouts  7.89 us (5%)
    pallas_call x1, Pallas kernels, fast_device(): pl.pallas_call(functools.partial(fused, energy), out_shape=(jax.ShapeDtyp...  146 us
    unnamed x10, local copies, waits for them, and re-layouts  5.13 us

profile of v1, /device:TPU:0, one launch (start us, length us, event | category | flops | bytes accessed | tf_op | source)
XLA Modules:
  0.0 154.2 jit_solution(9306533597527295235)
XLA Ops:
  0.6 0.0 copy-start.3
  0.6 0.0 copy-start.2
  0.7 2.8 %reshape.11.amps = bf16[8,256,512]{2,1,0:T(8,128)(2,1)S(1)} reshape(bf16[8,256,4,1,128]{4,2,3,1,0:T(4,128)(2,1)} %param.6) | data formatting | bytes 4194304 | tf_op jit(solution)/shard_map/reshape | solution.py:292
  3.4 0.0 copy-done.3
  3.4 0.0 copy-done.2
  3.4 0.0 copy-start
  3.4 2.2 %copy-done = bf16[2,1024,1024]{2,1,0:T(8,128)(2,1)S(1)} copy-done((bf16[2,1024,1024]{2,1,0:T(8,128)(2,1)S(1)}, bf16[2,1024,1024]{2,1,0:T(8,128)(2,1)}, u32[]{:S(2)}) %copy-start) | copy-done | bytes 4194328
  5.6 0.0 copy-start.1
  5.6 1.7 %copy-done.1 = bf16[4,1,128,2304]{3,2,1,0:T(8,128)(2,1)S(1)} copy-done((bf16[4,1,128,2304]{3,2,1,0:T(8,128)(2,1)S(1)}, bf16[4,1,128,2304]{3,2,1,0:T(8,128)(2,1)}, u32[]{:S(2)}) %copy-start.1) | copy-done | bytes 2359320
  7.3 145.6 %shard_map.68 = (f32[16,2048]{1,0:T(8,128)S(1)}, f32[16,512]{1,0:T(8,128)S(1)}) custom-call(s32[1,16]{1,0:T(1,128)S(1)} %copy-done.2, s32[16]{0:T(128)S(1)} %copy-done.3, bf16[4,128,2304]{2,1,0:T(8,128)(2,1)S(1)} %bitcast.3, bf16[8,256,512]{2,1,0:T(8,128)(2,1)S(1)} %reshape.11.amps, bf16[2,1024,1024]{2,1,0:T(8,128)(2,1)S(1)} %copy-done), custom_call_target="tpu_custom_call" | custom-call | tf_op jit(solution)/shard_map/pallas_call | solution.py:298
  152.9 0.7 copy.9
  153.6 0.6 copy.10
Async XLA Ops:
  0.6 2.8 %copy-start.3 = (s32[16]{0:T(128)S(1)}, s32[16]{0:T(128)}, u32[]{:S(2)}) copy-start(s32[16]{0:T(128)} %first.1) | copy-start | bytes 196
  0.6 2.8 %copy-start.2 = (s32[1,16]{1,0:T(1,128)S(1)}, s32[1,16]{1,0:T(1,128)}, u32[]{:S(2)}) copy-start(s32[1,16]{1,0:T(1,128)} %offs.1) | copy-start | bytes 196
  3.4 2.2 %copy-start = (bf16[2,1024,1024]{2,1,0:T(8,128)(2,1)S(1)}, bf16[2,1024,1024]{2,1,0:T(8,128)(2,1)}, u32[]{:S(2)}) copy-start(bf16[2,1024,1024]{2,1,0:T(8,128)(2,1)} %constant.2.clone.basis_hbm) | copy-start | bytes 12582916
  5.6 1.7 %copy-start.1 = (bf16[4,1,128,2304]{3,2,1,0:T(8,128)(2,1)S(1)}, bf16[4,1,128,2304]{3,2,1,0:T(8,128)(2,1)}, u32[]{:S(2)}) copy-start(bf16[4,1,128,2304]{3,2,1,0:T(8,128)(2,1)} %param.5) | copy-start | bytes 7077892

commit v2 on v1

--- a/solution.py
+++ b/solution.py
@@ -187,7 +187,7 @@
         x_copies[-1].start()
 
     carry[...] = jnp.zeros_like(carry)
-    lane0 = lax.broadcasted_iota(jnp.int32, (32, 128), 1) == 0
+    lanes = lax.broadcasted_iota(jnp.int32, (32, 128), 1)
     own_copy.wait()
 
     def delayed(j):
@@ -199,30 +199,32 @@
             d = jnp.dot(a, own[:, :, cols].reshape(4 * NAXIAL, CHUNK), preferred_element_type=jnp.float32)
             d = d + jnp.dot(a, following[:, :, cols].reshape(4 * NAXIAL, CHUNK), preferred_element_type=jnp.float32)
             d = d.reshape(KTAPS, 32, CHUNK)
-            total = d[KTAPS - 1]
-            for m in range(KTAPS - 2, -1, -1):
-                turned = pltpu.roll(total, 1, axis=1)
-                before = carry[m, rows, :]
-                carry[m, rows, :] = turned[:, :128]
-                lead = jnp.where(lane0, before, turned[:, :128])
-                total = d[m] + jnp.concatenate([lead, turned[:, 128:]], axis=1)
+            total = d[0]
+            for m in range(1, KTAPS):
+                turned = pltpu.roll(d[m], m, axis=1)
+                before = carry[m - 1, rows, :]
+                carry[m - 1, rows, :] = turned[:, :128]
+                lead = jnp.where(lanes < m, before, turned[:, :128])
+                total = total + jnp.concatenate([lead, turned[:, 128:]], axis=1)
             series[rows, cols] = 0.5 * total
             return 0
 
-        lax.fori_loop(0, NO // 32, body, 0)
+        lax.fori_loop(0, NO // 32, body, 0, unroll=2)
 
     def make_terms(q):
-        def body(b, _):
-            offset = offs[0, b]
-            shift = HEAD - jnp.maximum(offset, 0)
-            rows = pl.ds(pl.multiple_of(b * OBS, OBS), OBS)
-            part = series[rows, pl.ds(q * CHUNK, CHUNK + HEAD)]
-            part = moved(part, jnp.full((OBS, CHUNK + HEAD), shift, jnp.int32), 9, CHUNK)
-            part = jnp.where(jnp.full((OBS, CHUNK), offset, jnp.int32) >= 0, part, 0.0)
-            terms[q, lax.rem(b, 2), lax.rem(b // 2, 2), b // 4] = part
+        def body(level, _):
+            for place in range(4):
+                b = level * 4 + place
+                offset = offs[0, b]
+                shift = HEAD - jnp.maximum(offset, 0)
+                rows = pl.ds(pl.multiple_of(b * OBS, OBS), OBS)
+                part = series[rows, pl.ds(q * CHUNK, CHUNK + HEAD)]
+                part = pltpu.roll(part, CHUNK + HEAD - shift, axis=1)[:, :CHUNK]
+                part = jnp.where(jnp.full((OBS, CHUNK), offset, jnp.int32) >= 0, part, 0.0)
+                terms[q, place % 2, place // 2, level] = part
             return 0
 
-        lax.fori_loop(0, 16, body, 0)
+        lax.fori_loop(0, NZ, body, 0, unroll=2)
 
     c_copies, y_copies, z_copies = [], [], []
     for j in range(N_IN + 4):

time: 154 us -> 71.9 us (0.47)
  Pallas kernels: 146 us -> 63.1 us
    pallas_call x1, Pallas kernels: 146 us -> 63.1 us  [fast_device(): pl.pallas_call(functools.partial(fused, energy), out_shape=(jax.ShapeDtyp...]
where the time goes in v2:
time: 71.9 us; the launch traced here: 71.7 us
  Pallas kernels  63.1 us (88%)
  local copies, waits for them, and re-layouts  7.89 us (11%)
    pallas_call x1, Pallas kernels, fast_device(): pl.pallas_call(functools.partial(fused, energy), out_shape=(jax.ShapeDtyp...  63.1 us
    unnamed x10, local copies, waits for them, and re-layouts  5.13 us
    reshape x1, local copies, waits for them, and re-layouts, fast_device(): amps = amplitudes.reshape(KTAPS, NO, 4 * NAXIAL)  2.76 us

profile of v2, /device:TPU:0, one launch (start us, length us, event | category | flops | bytes accessed | tf_op | source)
XLA Modules:
  0.0 71.7 jit_solution(12567828424729671489)
XLA Ops:
  0.6 0.0 copy-start.3
  0.6 0.0 copy-start.2
  0.7 2.8 %reshape.11.amps = bf16[8,256,512]{2,1,0:T(8,128)(2,1)S(1)} reshape(bf16[8,256,4,1,128]{4,2,3,1,0:T(4,128)(2,1)} %param.6) | data formatting | bytes 4194304 | tf_op jit(solution)/shard_map/reshape | solution.py:294
  3.4 0.0 copy-done.3
  3.4 0.0 copy-done.2
  3.4 0.0 copy-start
  3.4 2.2 %copy-done = bf16[2,1024,1024]{2,1,0:T(8,128)(2,1)S(1)} copy-done((bf16[2,1024,1024]{2,1,0:T(8,128)(2,1)S(1)}, bf16[2,1024,1024]{2,1,0:T(8,128)(2,1)}, u32[]{:S(2)}) %copy-start) | copy-done | bytes 4194328
  5.6 0.0 copy-start.1
  5.6 1.7 %copy-done.1 = bf16[4,1,128,2304]{3,2,1,0:T(8,128)(2,1)S(1)} copy-done((bf16[4,1,128,2304]{3,2,1,0:T(8,128)(2,1)S(1)}, bf16[4,1,128,2304]{3,2,1,0:T(8,128)(2,1)}, u32[]{:S(2)}) %copy-start.1) | copy-done | bytes 2359320
  7.3 63.1 %shard_map.68 = (f32[16,2048]{1,0:T(8,128)S(1)}, f32[16,512]{1,0:T(8,128)S(1)}) custom-call(s32[1,16]{1,0:T(1,128)S(1)} %copy-done.2, s32[16]{0:T(128)S(1)} %copy-done.3, bf16[4,128,2304]{2,1,0:T(8,128)(2,1)S(1)} %bitcast.3, bf16[8,256,512]{2,1,0:T(8,128)(2,1)S(1)} %reshape.11.amps, bf16[2,1024,1024]{2,1,0:T(8,128)(2,1)S(1)} %copy-done), custom_call_target="tpu_custom_call" | custom-call | tf_op jit(solution)/shard_map/pallas_call | solution.py:300
  70.4 0.7 copy.9
  71.1 0.6 copy.10
Async XLA Ops:
  0.6 2.8 %copy-start.3 = (s32[16]{0:T(128)S(1)}, s32[16]{0:T(128)}, u32[]{:S(2)}) copy-start(s32[16]{0:T(128)} %first.1) | copy-start | bytes 196
  0.6 2.8 %copy-start.2 = (s32[1,16]{1,0:T(1,128)S(1)}, s32[1,16]{1,0:T(1,128)}, u32[]{:S(2)}) copy-start(s32[1,16]{1,0:T(1,128)} %offs.1) | copy-start | bytes 196
  3.4 2.2 %copy-start = (bf16[2,1024,1024]{2,1,0:T(8,128)(2,1)S(1)}, bf16[2,1024,1024]{2,1,0:T(8,128)(2,1)}, u32[]{:S(2)}) copy-start(bf16[2,1024,1024]{2,1,0:T(8,128)(2,1)} %constant.2.clone.basis_hbm) | copy-start | bytes 12582916
  5.6 1.7 %copy-start.1 = (bf16[4,1,128,2304]{3,2,1,0:T(8,128)(2,1)S(1)}, bf16[4,1,128,2304]{3,2,1,0:T(8,128)(2,1)}, u32[]{:S(2)}) copy-start(bf16[4,1,128,2304]{3,2,1,0:T(8,128)(2,1)} %param.5) | copy-start | bytes 7077892

commit v3 on v2

--- a/solution.py
+++ b/solution.py
@@ -113,6 +113,7 @@
 N_IN = NSRC // CHUNK
 N_OUT = NSAMP // CHUNK
 NZ = 4
+WINDOW = 2
 OBS = 16
 MESH = pl.DeviceIdType.MESH
 
@@ -184,7 +185,8 @@
     for j in range(N_IN):
         cols = pl.ds(j * CHUNK, CHUNK)
         x_copies.append(remote(nodes.at[:, :, cols], following.at[:, :, cols], x_send.at[j], x_recv.at[j], left))
-        x_copies[-1].start()
+        if j < WINDOW:
+            x_copies[j].start()
 
     carry[...] = jnp.zeros_like(carry)
     lanes = lax.broadcasted_iota(jnp.int32, (32, 128), 1)
@@ -229,6 +231,9 @@
     c_copies, y_copies, z_copies = [], [], []
     for j in range(N_IN + 4):
         if j < N_IN:
+            x_copies[j].wait_send()
+            if j + WINDOW < N_IN:
+                x_copies[j + WINDOW].start()
             x_copies[j].wait_recv()
             delayed(j)
         q = j - 1
@@ -284,7 +289,7 @@
             power = coeffs * coeffs if power is None else power + coeffs * coeffs
         spectra_out[:, pl.ds(f, CHUNK)] = (power[:OBS] + power[OBS:]) * (0.5 / energy)
 
-    for copy in x_copies + c_copies + y_copies + sum(z_copies, []):
+    for copy in c_copies + y_copies + sum(z_copies, []):
         copy.wait_send()
 
 
@@ -294,7 +299,7 @@
     amps = amplitudes.reshape(KTAPS, NO, 4 * NAXIAL)
     vmem = pl.BlockSpec(memory_space=pltpu.VMEM)
     smem = pl.BlockSpec(memory_space=pltpu.SMEM)
-    anywhere = pl.BlockSpec(memory_space=pl.ANY)
+    anywhere = pl.BlockSpec(memory_space=pltpu.HBM)
     dma = pltpu.SemaphoreType.DMA
     f32 = jnp.float32
     return pl.pallas_call(

time: 71.9 us -> 66.3 us (0.922)
  Pallas kernels: 63.1 us -> 57.5 us
    pallas_call x1, Pallas kernels: 63.1 us -> 57.5 us  [fast_device(): pl.pallas_call(functools.partial(fused, energy), out_shape=(jax.ShapeDtyp...]
where the time goes in v3:
time: 66.3 us; the launch traced here: 66.1 us
  Pallas kernels  57.5 us (87%)
  local copies, waits for them, and re-layouts  7.89 us (12%)
  between operations  0.69 us (1%)
    pallas_call x1, Pallas kernels, fast_device(): pl.pallas_call(functools.partial(fused, energy), out_shape=(jax.ShapeDtyp...  57.5 us
    unnamed x10, local copies, waits for them, and re-layouts  5.13 us
    reshape x1, local copies, waits for them, and re-layouts, fast_device(): amps = amplitudes.reshape(KTAPS, NO, 4 * NAXIAL)  2.76 us

profile of v3, /device:TPU:0, one launch (start us, length us, event | category | flops | bytes accessed | tf_op | source)
XLA Modules:
  0.0 66.1 jit_solution(15217991088091047483)
XLA Ops:
  0.6 0.0 copy-start.3
  0.6 0.0 copy-start.2
  0.7 2.8 %reshape.11.amps = bf16[8,256,512]{2,1,0:T(8,128)(2,1)S(1)} reshape(bf16[8,256,4,1,128]{4,2,3,1,0:T(4,128)(2,1)} %param.6) | data formatting | bytes 4194304 | tf_op jit(solution)/shard_map/reshape | solution.py:299
  3.4 0.0 copy-done.3
  3.4 0.0 copy-done.2
  3.4 0.0 copy-start
  3.4 2.2 %copy-done = bf16[2,1024,1024]{2,1,0:T(8,128)(2,1)S(1)} copy-done((bf16[2,1024,1024]{2,1,0:T(8,128)(2,1)S(1)}, bf16[2,1024,1024]{2,1,0:T(8,128)(2,1)}, u32[]{:S(2)}) %copy-start) | copy-done | bytes 4194328
  5.6 0.0 copy-start.1
  5.6 1.7 %copy-done.1 = bf16[4,1,128,2304]{3,2,1,0:T(8,128)(2,1)S(1)} copy-done((bf16[4,1,128,2304]{3,2,1,0:T(8,128)(2,1)S(1)}, bf16[4,1,128,2304]{3,2,1,0:T(8,128)(2,1)}, u32[]{:S(2)}) %copy-start.1) | copy-done | bytes 2359320
  7.3 57.5 %shard_map.68 = (f32[16,2048]{1,0:T(8,128)S(1)}, f32[16,512]{1,0:T(8,128)S(1)}) custom-call(s32[1,16]{1,0:T(1,128)S(1)} %copy-done.2, s32[16]{0:T(128)S(1)} %copy-done.3, bf16[4,128,2304]{2,1,0:T(8,128)(2,1)S(1)} %bitcast.3, bf16[8,256,512]{2,1,0:T(8,128)(2,1)S(1)} %reshape.11.amps, bf16[2,1024,1024]{2,1,0:T(8,128)(2,1)S(1)} %copy-done), custom_call_target="tpu_custom_call" | custom-call | tf_op jit(solution)/shard_map/pallas_call | solution.py:305
  64.8 0.7 copy.9
  65.5 0.6 copy.10
Async XLA Ops:
  0.6 2.8 %copy-start.3 = (s32[16]{0:T(128)S(1)}, s32[16]{0:T(128)}, u32[]{:S(2)}) copy-start(s32[16]{0:T(128)} %first.1) | copy-start | bytes 196
  0.6 2.8 %copy-start.2 = (s32[1,16]{1,0:T(1,128)S(1)}, s32[1,16]{1,0:T(1,128)}, u32[]{:S(2)}) copy-start(s32[1,16]{1,0:T(1,128)} %offs.1) | copy-start | bytes 196
  3.4 2.2 %copy-start = (bf16[2,1024,1024]{2,1,0:T(8,128)(2,1)S(1)}, bf16[2,1024,1024]{2,1,0:T(8,128)(2,1)}, u32[]{:S(2)}) copy-start(bf16[2,1024,1024]{2,1,0:T(8,128)(2,1)} %constant.2.clone.basis_hbm) | copy-start | bytes 12582916
  5.6 1.7 %copy-start.1 = (bf16[4,1,128,2304]{3,2,1,0:T(8,128)(2,1)S(1)}, bf16[4,1,128,2304]{3,2,1,0:T(8,128)(2,1)}, u32[]{:S(2)}) copy-start(bf16[4,1,128,2304]{3,2,1,0:T(8,128)(2,1)} %param.5) | copy-start | bytes 7077892

commit v4 on v3

--- a/solution.py
+++ b/solution.py
@@ -211,7 +211,7 @@
             series[rows, cols] = 0.5 * total
             return 0
 
-        lax.fori_loop(0, NO // 32, body, 0, unroll=2)
+        lax.fori_loop(0, NO // 32, body, 0, unroll=4)
 
     def make_terms(q):
         def body(level, _):
@@ -226,7 +226,7 @@
                 terms[q, place % 2, place // 2, level] = part
             return 0
 
-        lax.fori_loop(0, NZ, body, 0, unroll=2)
+        lax.fori_loop(0, NZ, body, 0, unroll=4)
 
     c_copies, y_copies, z_copies = [], [], []
     for j in range(N_IN + 4):

time: 66.3 us -> 65.5 us (0.988)
  Pallas kernels: 57.5 us -> 56.7 us
    pallas_call x1, Pallas kernels: 57.5 us -> 56.7 us  [fast_device(): pl.pallas_call(functools.partial(fused, energy), out_shape=(jax.ShapeDtyp...]
where the time goes in v4:
time: 65.5 us; the launch traced here: 65.2 us
  Pallas kernels  56.7 us (87%)
  local copies, waits for them, and re-layouts  7.89 us (12%)
  between operations  0.69 us (1%)
    pallas_call x1, Pallas kernels, fast_device(): pl.pallas_call(functools.partial(fused, energy), out_shape=(jax.ShapeDtyp...  56.7 us
    unnamed x10, local copies, waits for them, and re-layouts  5.13 us
    reshape x1, local copies, waits for them, and re-layouts, fast_device(): amps = amplitudes.reshape(KTAPS, NO, 4 * NAXIAL)  2.76 us

profile of v4, /device:TPU:0, one launch (start us, length us, event | category | flops | bytes accessed | tf_op | source)
XLA Modules:
  0.0 65.2 jit_solution(12352401981877420507)
XLA Ops:
  0.6 0.0 copy-start.3
  0.6 0.0 copy-start.2
  0.7 2.8 %reshape.11.amps = bf16[8,256,512]{2,1,0:T(8,128)(2,1)S(1)} reshape(bf16[8,256,4,1,128]{4,2,3,1,0:T(4,128)(2,1)} %param.6) | data formatting | bytes 4194304 | tf_op jit(solution)/shard_map/reshape | solution.py:299
  3.4 0.0 copy-done.3
  3.4 0.0 copy-done.2
  3.4 0.0 copy-start
  3.4 2.2 %copy-done = bf16[2,1024,1024]{2,1,0:T(8,128)(2,1)S(1)} copy-done((bf16[2,1024,1024]{2,1,0:T(8,128)(2,1)S(1)}, bf16[2,1024,1024]{2,1,0:T(8,128)(2,1)}, u32[]{:S(2)}) %copy-start) | copy-done | bytes 4194328
  5.6 0.0 copy-start.1
  5.6 1.7 %copy-done.1 = bf16[4,1,128,2304]{3,2,1,0:T(8,128)(2,1)S(1)} copy-done((bf16[4,1,128,2304]{3,2,1,0:T(8,128)(2,1)S(1)}, bf16[4,1,128,2304]{3,2,1,0:T(8,128)(2,1)}, u32[]{:S(2)}) %copy-start.1) | copy-done | bytes 2359320
  7.3 56.7 %shard_map.68 = (f32[16,2048]{1,0:T(8,128)S(1)}, f32[16,512]{1,0:T(8,128)S(1)}) custom-call(s32[1,16]{1,0:T(1,128)S(1)} %copy-done.2, s32[16]{0:T(128)S(1)} %copy-done.3, bf16[4,128,2304]{2,1,0:T(8,128)(2,1)S(1)} %bitcast.3, bf16[8,256,512]{2,1,0:T(8,128)(2,1)S(1)} %reshape.11.amps, bf16[2,1024,1024]{2,1,0:T(8,128)(2,1)S(1)} %copy-done), custom_call_target="tpu_custom_call" | custom-call | tf_op jit(solution)/shard_map/pallas_call | solution.py:305
  64.0 0.7 %copy.9 = f32[16,2048]{1,0:T(8,128)} copy(f32[16,2048]{1,0:T(8,128)S(1)} %get-tuple-element.4) | data formatting | bytes 262144
  64.6 0.6 copy.10
Async XLA Ops:
  0.6 2.8 %copy-start.3 = (s32[16]{0:T(128)S(1)}, s32[16]{0:T(128)}, u32[]{:S(2)}) copy-start(s32[16]{0:T(128)} %first.1) | copy-start | bytes 196
  0.6 2.8 %copy-start.2 = (s32[1,16]{1,0:T(1,128)S(1)}, s32[1,16]{1,0:T(1,128)}, u32[]{:S(2)}) copy-start(s32[1,16]{1,0:T(1,128)} %offs.1) | copy-start | bytes 196
  3.4 2.2 %copy-start = (bf16[2,1024,1024]{2,1,0:T(8,128)(2,1)S(1)}, bf16[2,1024,1024]{2,1,0:T(8,128)(2,1)}, u32[]{:S(2)}) copy-start(bf16[2,1024,1024]{2,1,0:T(8,128)(2,1)} %constant.2.clone.basis_hbm) | copy-start | bytes 12582916
  5.6 1.7 %copy-start.1 = (bf16[4,1,128,2304]{3,2,1,0:T(8,128)(2,1)S(1)}, bf16[4,1,128,2304]{3,2,1,0:T(8,128)(2,1)}, u32[]{:S(2)}) copy-start(bf16[4,1,128,2304]{3,2,1,0:T(8,128)(2,1)} %param.5) | copy-start | bytes 7077892
